TPU v7x, 1024 devices: a whole 4x8x16 slice. The times are simulated.
1024 devices in a mesh: dp: 4 (over x), expert: 16 (over z), tensor: 16 (over y, core).
Axes of the slice: x: 4, y: 8, z: 16, core: 2. Of those that a mesh axis runs over, the one named last changes fastest.
Arguments:
- grad_out: bfloat16 [8192, 7168], P(('dp', 'expert'), 'tensor'), may hold values from -6 to 6
- route_ids: int32 [8192, 2], P(('dp', 'expert')), may hold values from 0 to 15, all different within a row; in each aligned block of 128 rows (0 to 127, 128 to 255, ...) at most 24 rows name the same one
- route_gates: float32 [8192, 2], P(('dp', 'expert')), may hold values from 0.05 to 1
- hidden_acts: bfloat16 [4, 16, 384, 4864], P('dp', 'expert'), may hold values from -0.29882812 to 0.29882812
- down_weight: bfloat16 [16, 4864, 7168], P('expert', None, 'tensor'), may hold values from -0.078125 to 0.078125
Outputs:
- grad_weight: bfloat16 [16, 4864, 7168], P('expert', 'dp', 'tensor')
- grad_hidden: bfloat16 [4, 16, 384, 4864], P('dp', 'expert', None, 'tensor')
Inputs may be any that keep to these rules, and one draw needn't show every extreme that they name: `route_ids`: in each aligned block of 128 rows (the tokens of one group) no expert is named by more than 24 rows, a bound that some block reaches; the two experts of a row differ.
All inputs are finite; a program needn't handle non-finite values.
Results may differ from a plain program's by a relative error of at most 0.022.
Values may be sent and summed in bfloat16 or wider, within the bound.
A program may use at most 64 MiB of HBM per device.

v0:
```python
import jax
import jax.numpy as jnp
from jax import lax
from jax.sharding import PartitionSpec as P


def rounded(product):
    return lax.optimization_barrier(product.astype(jnp.bfloat16)).astype(jnp.float32)


def on_device(grad_out, route_ids, route_gates, hidden_acts, down_weight):
    experts_here = lax.axis_size("expert")
    tok_rows = grad_out.shape[0]
    slot_count = hidden_acts.shape[2]
    capacity = slot_count // experts_here
    ids_flat = route_ids.reshape(-1)
    onehot = (ids_flat[:, None] == jnp.arange(experts_here, dtype=jnp.int32)[None, :]).astype(
        jnp.int32
    )
    before = jnp.cumsum(onehot, axis=0) - onehot
    slot_index = jnp.sum(before * onehot, axis=1)
    target = (ids_flat * capacity + slot_index).reshape(tok_rows, 2)
    places = jnp.arange(experts_here * capacity, dtype=jnp.int32)[:, None]
    placing = jnp.where(places == target[None, :, 0], route_gates[None, :, 0], 0.0)
    placing = placing + jnp.where(places == target[None, :, 1], route_gates[None, :, 1], 0.0)
    outgoing = jnp.dot(placing, grad_out.astype(jnp.float32), precision=lax.Precision.HIGHEST)
    outgoing = outgoing.astype(jnp.bfloat16).reshape(experts_here, capacity, grad_out.shape[1])
    arrived = lax.all_to_all(outgoing, "expert", split_axis=0, concat_axis=0, tiled=True).reshape(
        slot_count, grad_out.shape[1]
    )
    activations = hidden_acts[0, 0]
    weight = down_weight[0]
    product = lax.dot_general(
        weight, arrived, (((1,), (1,)), ((), ())), preferred_element_type=jnp.float32
    )
    shares = lax.psum_scatter(
        rounded(product).astype(jnp.bfloat16), "tensor", scatter_dimension=0, tiled=True
    ).astype(jnp.float32)
    grad_hidden = jnp.transpose(shares).astype(jnp.bfloat16)[None, None]
    product = lax.dot_general(
        activations, arrived, (((0,), (0,)), ((), ())), preferred_element_type=jnp.float32
    )
    summed = lax.psum_scatter(
        rounded(product).astype(jnp.bfloat16), "dp", scatter_dimension=0, tiled=True
    )
    grad_weight = summed[None]
    return (grad_weight, grad_hidden)


def solution(mesh):
    return jax.shard_map(
        on_device,
        mesh=mesh,
        in_specs=(
            P(("dp", "expert"), "tensor"),
            P(("dp", "expert"), None),
            P(("dp", "expert"), None),
            P("dp", "expert", None, None),
            P("expert", None, "tensor"),
        ),
        out_specs=(P("expert", "dp", "tensor"), P("dp", "expert", None, "tensor")),
        check_vma=False,
    )
```

profile of v0, /device:TPU:1, one launch (start us, length us, event | category | flops | bytes accessed | tf_op | source)
XLA Modules:
  0.0 208.2 jit_solution(5645536289164754055)
XLA Ops:
  7.2 0.0 copy-start
  7.2 0.0 reduce-scatter.9.cloned.1.call-start
  7.2 0.8 copy.29
  8.0 0.1 eq.60
  8.2 0.1 eq.56
  8.3 0.8 slice_bitcast_fusion.2
  9.1 0.6 reduce-window.6
  9.6 0.2 slice_reduce_fusion
  9.9 0.1 fusion.14
  10.0 0.1 reduce_sum.12
  10.1 0.1 copy.32
  10.2 0.7 multiply_add_fusion
  10.9 0.0 copy-done
  10.9 0.5 convolution_convert_fusion.2
  11.4 0.2 copy.33
  11.6 37.2 %all_to_all.5 = bf16[16,24,448]{2,1,0:T(8,128)(2,1)S(1)} all-to-all(bf16[16,24,448]{2,1,0:T(8,128)(2,1)S(1)} %bitcast.50), channel_id=1, replica_groups=mesh['dp'=4,'expert'=16,'tensor'=16] {'expert'}, dimensions={0} | all-to-all | bytes 688128 | tf_op jit(solution)/shard_map/all_to_all | solution.py:28
  48.8 6.1 %fusion.1 = bf16[4864,384]{0,1:T(8,128)(2,1)} fusion(bf16[384,448]{1,0:T(8,128)(2,1)S(1)} %bitcast.48, bf16[1,4864,448]{1,2,0:T(8,128)(2,1)} %param.9), kind=kOutput, calls=%fused_computation.3 | convolution fusion | flops 1675395072 | bytes 8437760 | tf_op jit(solution)/shard_map/dot_general | solution.py:33
  54.9 6.0 %copy.37 = bf16[4864,384]{1,0:T(8,128)(2,1)} copy(bf16[4864,384]{0,1:T(8,128)(2,1)} %fusion.1) | data formatting | bytes 7471104
  61.0 0.0 reduce-scatter.9.cloned.1.call-update
  61.0 0.0 reduce-scatter.7.cloned.1.call-start
  61.0 6.6 %fusion = bf16[4864,448]{0,1:T(8,128)(2,1)} fusion(bf16[384,448]{1,0:T(8,128)(2,1)S(1)} %bitcast.49, bf16[1,1,384,4864]{3,2,1,0:T(8,128)(2,1)} %param.8), kind=kOutput, calls=%fused_computation.2 | convolution fusion | flops 1675706368 | bytes 8437760 | tf_op jit(solution)/shard_map/dot_general | solution.py:40
  67.6 7.3 %copy.35 = bf16[4864,448]{1,0:T(8,128)(2,1)} copy(bf16[4864,448]{0,1:T(8,128)(2,1)} %fusion) | data formatting | bytes 8716288
  74.9 0.0 reduce-scatter.7.cloned.1.call-update
  75.0 56.3 %reduce-scatter.9.cloned.1.call-done = bf16[304,384]{1,0:T(8,128)(2,1)} async-done(((bf16[4864,384]{1,0:T(8,128)(2,1)}), bf16[304,384]{1,0:T(8,128)(2,1)}) %reduce-scatter.9.cloned.1.call-update) | async-done | bytes 233488
  131.2 1.1 copy.38
  132.4 0.9 copy.34
  133.2 65.7 %reduce-scatter.7.cloned.1.call-done = bf16[1216,448]{1,0:T(8,128)(2,1)} async-done(((bf16[4864,448]{1,0:T(8,128)(2,1)}), bf16[1216,448]{1,0:T(8,128)(2,1)}) %reduce-scatter.7.cloned.1.call-update) | async-done | bytes 1089552
  198.9 2.4 %copy.36 = bf16[1216,448]{0,1:T(8,128)(2,1)} copy(bf16[1216,448]{1,0:T(8,128)(2,1)} %reduce-scatter.7.cloned.1.call-done) | data formatting | bytes 2179072
  (4 shorter events, 0.1 us)
Async XLA Ops:
  7.2 3.7 %copy-start = (bf16[128,448]{0,1:T(8,128)(2,1)S(1)}, bf16[128,448]{0,1:T(8,128)(2,1)}, u32[]{:S(2)}) copy-start(bf16[128,448]{0,1:T(8,128)(2,1)} %param.5) | copy-start | bytes 344068
  7.2 124.0 %reduce-scatter.9.cloned.1.call-start = ((), (), s32[]{:S(2)}) async-start(), calls=%async_computation.4 | async-start | bytes 3969024
  61.0 137.9 %reduce-scatter.7.cloned.1.call-start = ((), (), s32[]{:S(2)}) async-start(), calls=%async_computation.3 | async-start | bytes 6225920
Sparse Core Ops, SparseCore 0:
  61.1 70.0 reduce-scatter.8
  135.0 63.8 reduce-scatter.6
where the time goes:
time: 209 us; the launch traced here: 208 us
  waiting for transfers between devices  122 us (58%)
  blocking collectives  37.2 us (18%)
  local copies, waits for them, and re-layouts  20.2 us (10%)
  between operations  14.1 us (7%)
  matrix products  13.2 us (6%)
    unnamed x4, waiting for transfers between devices  122 us
    all_to_all x1, blocking collectives, on_device(): lax.all_to_all(outgoing, 'expert', split_axis=0, concat_axis=0, tiled=True)  37.2 us
    unnamed x8, local copies, waits for them, and re-layouts  18.6 us
    dot_general x1, matrix products, on_device(): lax.dot_general(activations, arrived, (((0,), (0,)), ((), ())), preferred...  6.57 us
    dot_general x1, matrix products, on_device(): lax.dot_general(weight, arrived, (((1,), (1,)), ((), ())), preferred_elem...  6.14 us
  transfers between devices with their start and end apart: 2, of which 2 were waited for; matrix products, arithmetic and copies ran while one was open for 8% of the time, Pallas kernels for 0%

commit v1 on v0

v1 whole, which is shorter than its diff:
```python
import jax
import jax.numpy as jnp
from jax import lax
from jax.experimental import pallas as pl
from jax.experimental.pallas import tpu as pltpu
from jax.sharding import PartitionSpec as P

BF, F32 = jnp.bfloat16, jnp.float32
MESH = pl.DeviceIdType.MESH
HOPS = (0, 1, -1, 2, -2, 3, -3, 4, -4, 5, -5, 6, -6, 7, -7, 8)
TURNS = (4, 3, -3, 2, -2, 1, -1, 0)
GROUPS = ((0, 256), (256, 128))
CAP = 24


def dot(a, b, dims=((1,), (0,))):
    return lax.dot_general(a, b, (dims, ((), ())), preferred_element_type=F32)


def kernel(
    ids, gates, grad_t, acts, weight_t, gw_out, gh_out,
    staged, weight, acts_buf, fwd, outgoing, arrived, rows32, named, perm, total,
    rt0, rt1, peers0, peers1, own0, own1, give0, give1, take0, take1,
    pa0, pa1, pb0, pb1, ma0, ma1, mb0, mb1,
    send_sems, recv_sems, local_sems,
):
    nx, nz, nt = lax.axis_size("dp"), lax.axis_size("expert"), lax.axis_size("tensor")
    ny = nt // 2
    x, z, t = lax.axis_index("dp"), lax.axis_index("expert"), lax.axis_index("tensor")
    core = lax.rem(t, 2)
    y = lax.div(t, 2)
    right, left = {"dp": lax.rem(x + 1, nx)}, {"dp": lax.rem(x + nx - 1, nx)}
    up, down = {"tensor": lax.rem(t + 2, nt)}, {"tensor": lax.rem(t + nt - 2, nt)}
    twin = {"tensor": t + 1 - 2 * core}
    chunk = weight.shape[0] // nt
    part_a = (chunk // 2 + 15) // 16 * 16
    rows_a, rows_b = pl.ds(0, part_a), pl.ds(part_a, chunk - part_a)
    rt, peers, own, give, take = (rt0, rt1), (peers0, peers1), (own0, own1), (give0, give1), (take0, take1)
    pa, pb, ma, mb = (pa0, pa1), (pb0, pb1), (ma0, ma1), (mb0, mb1)
    count = [0]
    started = []

    def remote(src, dst, device):
        n = count[0]
        count[0] += 1
        return pltpu.make_async_remote_copy(
            src_ref=src, dst_ref=dst, send_sem=send_sems.at[n], recv_sem=recv_sems.at[n],
            device_id=device, device_id_type=MESH,
        )

    def start(copy):
        copy.start()
        started.append(copy)

    width = acts_buf.shape[3]
    load_weight = pltpu.make_async_copy(weight_t, staged, local_sems.at[0])
    load_weight.start()

    def column(owner, half):
        return pl.multiple_of((19 * owner // 2) * 128 + half * width, 128)

    loads = []
    for half in range(2):
        load = pltpu.make_async_copy(acts.at[:, pl.ds(column(x, half), width)], acts_buf.at[0, half], local_sems.at[1 + half])
        load.start()
        loads.append(load)

    barrier = pltpu.get_barrier_semaphore()
    experts = [lax.rem(z + nz - h, nz) for h in HOPS]
    greeted = [right, left, up, down, twin] + [{"expert": e} for e in experts[1:]]
    for device in greeted:
        pl.semaphore_signal(barrier, inc=1, device_id=device, device_id_type=MESH)

    id0, id1 = ids[0:1, :], ids[1:2, :]
    gate0, gate1 = gates[0:1, :], gates[1:2, :]
    tokens = ids.shape[1]
    for j, e in enumerate(experts):
        named[j : j + 1, :] = ((id0 == e) | (id1 == e)).astype(F32)
    earlier = lax.broadcasted_iota(jnp.int32, (tokens, tokens), 0) < lax.broadcasted_iota(jnp.int32, (tokens, tokens), 1)
    slots = dot(named[...].astype(BF), earlier.astype(F32).astype(BF)).astype(jnp.int32)
    place = lax.broadcasted_iota(jnp.int32, (CAP, tokens), 0)
    picks, scales = [], []
    for j, e in enumerate(experts):
        here = (slots[j : j + 1, :] == place) & (named[j : j + 1, :] > 0.5)
        gate = jnp.where(id0 == e, gate0, 0.0) + jnp.where(id1 == e, gate1, 0.0)
        picks.append(jnp.where(here, 1.0, 0.0))
        scales.append(jnp.sum(jnp.where(here, gate, 0.0), axis=1, keepdims=True))
    pick = jnp.concatenate(picks, axis=0).astype(BF)
    features = grad_t.shape[0]
    padded = rows32.shape[1]
    padded_grad = jnp.concatenate([grad_t[...], jnp.zeros((padded - features, tokens), BF)], axis=0)
    rows32[...] = dot(pick, padded_grad, ((1,), (1,))) * jnp.concatenate(scales, axis=0)
    lanes = padded // 128
    for j in range(nz):
        block = jnp.concatenate([rows32[CAP * j : CAP * (j + 1), 128 * i : 128 * (i + 1)] for i in range(lanes)], axis=0)
        if j == 0:
            arrived[0] = block.astype(BF)
        else:
            outgoing[j] = block.astype(BF)

    pl.semaphore_wait(barrier, len(greeted))

    to_expert = [None] + [remote(outgoing.at[j], arrived.at[j], {"expert": experts[j]}) for j in range(1, nz)]
    for copy in to_expert[1:]:
        start(copy)

    rows_here = acts.shape[0] // 2
    quarter = rows_here // 2
    first = pl.multiple_of(lax.rem(y, 2) * rows_here, 16)
    other = pl.multiple_of((1 - lax.rem(y, 2)) * rows_here, 16)
    far = lax.rem(x + 2, nx)
    x_near = []
    for q, device, owner in ((1, right, lax.rem(x + 1, nx)), (2, left, lax.rem(x + nx - 1, nx))):
        x_near.append(remote(
            acts.at[pl.ds(first, rows_here), pl.ds(column(owner, core), width)],
            acts_buf.at[q, core, pl.ds(first, rows_here), :], device,
        ))
    x_half, x_far = [], []
    for k, device in ((0, right), (1, left)):
        here = pl.ds(pl.multiple_of(first + k * quarter, 16), quarter)
        x_half.append(remote(acts.at[here, pl.ds(column(far, core), width)], fwd.at[k], device))
        x_far.append(remote(fwd.at[k], acts_buf.at[3, core, here, :], device))
    for copy in x_near + x_half:
        start(copy)
    y_part, twin_part = {}, {}
    for q in (1, 2, 3):
        for k, device in ((0, up), (1, down)):
            here = acts_buf.at[q, core, pl.ds(pl.multiple_of(first + k * quarter, 16), quarter), :]
            there = acts_buf.at[q, core, pl.ds(pl.multiple_of(other + k * quarter, 16), quarter), :]
            y_part[q, k] = remote(here, here, device)
            twin_part[q, k] = remote(there, there, twin)
        here = acts_buf.at[q, core, pl.ds(first, rows_here), :]
        twin_part[q, 2] = remote(here, here, twin)

    load_weight.wait()

    def turn(i, carry):
        at = pl.multiple_of(i * 128, 128)
        weight[pl.ds(at, 128), :] = staged[:, pl.ds(at, 128)].astype(F32).T.astype(BF)
        return carry

    lax.fori_loop(0, weight.shape[0] // 128, turn, 0)

    slot_count = perm.shape[1]
    stands = lax.broadcasted_iota(jnp.int32, (CAP, slot_count), 1) - lax.broadcasted_iota(jnp.int32, (CAP, slot_count), 0)
    perm[...] = jnp.concatenate(
        [jnp.where(stands == CAP * lax.rem(z + nz + h, nz), 1.0, 0.0) for h in HOPS], axis=0
    ).astype(BF)

    def near_acts():
        for q in (1, 2):
            x_near[q - 1].wait_recv()
            start(y_part[q, 0])
            start(y_part[q, 1])
            start(twin_part[q, 2])

    def half_acts():
        for k in range(2):
            x_half[k].wait_recv()
            start(x_far[k])

    def far_acts():
        for k in range(2):
            x_far[k].wait_recv()
            start(y_part[3, k])
        start(twin_part[3, 2])

    def shared_acts(q):
        for k in range(2):
            y_part[q, k].wait_recv()
            start(twin_part[q, k])

    to_peers = []
    for g, (low, size) in enumerate(GROUPS):
        top, bottom = pl.ds(0, features // 2), pl.ds(features // 2, features // 2)
        to_peers.append((
            remote(rt[g], peers[g].at[0], right),
            remote(rt[g], peers[g].at[1], left),
            remote(peers[g].at[0, top, :], peers[g].at[2, top, :], right),
            remote(peers[g].at[1, bottom, :], peers[g].at[2, bottom, :], left),
        ))
    unpacked = [0]

    def collect(g):
        low, size = GROUPS[g]
        until = -(-(low + size) // CAP)
        for j in range(unpacked[0], until):
            if j:
                to_expert[j].wait_recv()
            block = arrived[j].astype(F32)
            for i in range(lanes):
                rows32[CAP * j : CAP * (j + 1), 128 * i : 128 * (i + 1)] = block[CAP * i : CAP * (i + 1), :]
        unpacked[0] = until
        rt[g][...] = rows32[low : low + size, :].T[:features, :].astype(BF)
        start(to_peers[g][0])
        start(to_peers[g][1])

    def pass_on(g):
        for k in range(2):
            to_peers[g][k].wait_recv()
            start(to_peers[g][2 + k])

    index = {turn_: i for i, turn_ in enumerate(TURNS)}
    index[-4] = index[4]
    to_twin, rings = [], []
    for g in range(len(GROUPS)):
        to_twin.append([remote(give[g].at[i], take[g].at[i], twin) for i in range(ny)])
        ring = {}
        for s in range(4):
            ring["pa", s] = remote(own[g].at[index[4 - s], rows_a, :], pa[g].at[s], up)
            ring["mb", s] = remote(own[g].at[index[s - 4], rows_b, :], mb[g].at[s], down)
        for s in range(3):
            ring["pb", s] = remote(own[g].at[index[3 - s], rows_b, :], pb[g].at[s], up)
            ring["ma", s] = remote(own[g].at[index[s - 3], rows_a, :], ma[g].at[s], down)
        rings.append(ring)

    def product(g, i, side):
        at = pl.multiple_of(chunk * (2 * lax.rem(y + ny + TURNS[i], ny) + side), 16)
        return dot(weight[pl.ds(at, chunk), :], rt[g][...]).astype(BF)

    def prepare(g, *which):
        for i in which:
            give[g][i] = product(g, i, 1 - core)
            start(to_twin[g][i])
            own[g][i] = product(g, i, core)

    def join(g, *which):
        for i in which:
            to_twin[g][i].wait_recv()
            own[g][i] = (own[g][i].astype(F32) + take[g][i].astype(F32)).astype(BF)

    def step(g, name, s):
        ring = rings[g]
        ring[name, s].wait_recv()
        buffer = {"pa": pa, "pb": pb, "ma": ma, "mb": mb}[name][g]
        rows = rows_a if name[1] == "a" else rows_b
        reach = {"pa": 3 - s, "pb": 2 - s, "ma": s - 2, "mb": s - 3}[name]
        i = index[reach]
        own[g][i, rows, :] = (own[g][i, rows, :].astype(F32) + buffer[s].astype(F32)).astype(BF)
        start(ring[name, s + 1])

    def stage0(g):
        prepare(g, 0, 1, 2)
        join(g, 0)
        start(rings[g]["pa", 0])
        start(rings[g]["mb", 0])
        join(g, 1, 2)
        start(rings[g]["pb", 0])
        start(rings[g]["ma", 0])

    def stage1(g):
        prepare(g, 3, 4)
        join(g, 3, 4)
        for name in ("pa", "mb", "pb", "ma"):
            step(g, name, 0)

    def stage2(g):
        prepare(g, 5, 6)
        join(g, 5, 6)
        for name in ("pa", "mb", "pb", "ma"):
            step(g, name, 1)

    def stage3(g):
        prepare(g, 7)
        join(g, 7)
        step(g, "pa", 2)
        step(g, "mb", 2)

    def finish(g):
        low, size = GROUPS[g]
        ring = rings[g]
        for name, s in (("pb", 2), ("ma", 2), ("pa", 3), ("mb", 3)):
            ring[name, s].wait_recv()
        i = index[0]
        share_a = own[g][i, rows_a, :].astype(F32) + (pa[g][3].astype(F32) + ma[g][2].astype(F32))
        share_b = own[g][i, rows_b, :].astype(F32) + (pb[g][2].astype(F32) + mb[g][3].astype(F32))
        return jnp.concatenate([share_a, share_b], axis=0).astype(BF)

    def weight_grad(q):
        both = [r[...] for r in rt] if q == 0 else [r[q - 1] for r in peers]
        ordered = sum(dot(b, perm[low : low + size, :]) for b, (low, size) in zip(both, GROUPS)).astype(BF)
        for half in range(2):
            columns = pl.ds(half * width, width)
            added = dot(ordered, acts_buf[q, half])
            if q == 0:
                total[:, columns] = added
            elif q < 3:
                total[:, columns] += added
            else:
                gw_out[:, columns] = (total[:, columns] + added).astype(BF)

    near_acts()
    half_acts()
    collect(0)
    stage0(0)
    far_acts()
    stage1(0)
    shared_acts(1)
    shared_acts(2)
    stage2(0)
    pass_on(0)
    collect(1)
    prepare(1, 0, 1, 2)
    stage3(0)
    join(1, 0)
    start(rings[1]["pa", 0])
    start(rings[1]["mb", 0])
    join(1, 1, 2)
    start(rings[1]["pb", 0])
    start(rings[1]["ma", 0])
    shared_acts(3)
    pass_on(1)
    stage1(1)
    done0 = finish(0)
    gh = dot(done0, perm[0 : GROUPS[0][1], :])
    stage2(1)
    for load in loads:
        load.wait()
    weight_grad(0)
    stage3(1)
    for q in (1, 2):
        for k in range(3):
            twin_part[q, k].wait_recv()
        weight_grad(q)
    done1 = finish(1)
    gh_out[...] = (gh + dot(done1, perm[GROUPS[1][0] :, :])).astype(BF)
    for k in range(3):
        twin_part[3, k].wait_recv()
    for g in range(len(GROUPS)):
        for k in range(2):
            to_peers[g][2 + k].wait_recv()
    weight_grad(3)
    for copy in started:
        copy.wait_send()


def routed_backward(ids, gates, grad_t, acts, weight_t):
    features, hidden = weight_t.shape
    slots = acts.shape[0]
    nx, nz, nt = lax.axis_size("dp"), lax.axis_size("expert"), lax.axis_size("tensor")
    width, chunk = 640, hidden // nt
    part_a = (chunk // 2 + 15) // 16 * 16
    part_b = chunk - part_a
    padded = -(-features // 128) * 128
    block = CAP * padded // 128
    sizes = [size for _, size in GROUPS]
    vmem = pltpu.VMEM
    scratch = [
        vmem((features, hidden), BF),
        vmem((hidden, features), BF),
        vmem((nx, 2, slots, width), BF),
        vmem((2, slots // 4, width), BF),
        vmem((nz, block, 128), BF),
        vmem((nz, block, 128), BF),
        vmem((slots, padded), F32),
        vmem((nz, ids.shape[1]), F32),
        vmem((slots, slots), BF),
        vmem((features, 2 * width), F32),
    ]
    scratch += [vmem((features, n), BF) for n in sizes]
    scratch += [vmem((3, features, n), BF) for n in sizes]
    for _ in range(3):
        scratch += [vmem((nt // 2, chunk, n), BF) for n in sizes]
    for hops, rows in ((4, part_a), (3, part_b), (3, part_a), (4, part_b)):
        scratch += [vmem((hops, rows, n), BF) for n in sizes]
    copies = (nz - 1) + 6 + 15 + 8 + 2 * (nt // 2 + 14)
    scratch += [
        pltpu.SemaphoreType.DMA((copies,)),
        pltpu.SemaphoreType.DMA((copies,)),
        pltpu.SemaphoreType.DMA((3,)),
    ]
    whole = pl.BlockSpec(memory_space=pltpu.VMEM)
    away = pl.BlockSpec(memory_space=pl.ANY)
    return pl.pallas_call(
        kernel,
        out_shape=(
            jax.ShapeDtypeStruct((features, 2 * width), BF),
            jax.ShapeDtypeStruct((chunk, slots), BF),
        ),
        in_specs=[whole, whole, whole, away, away],
        out_specs=(whole, whole),
        scratch_shapes=scratch,
        compiler_params=pltpu.CompilerParams(
            collective_id=0, has_side_effects=True, vmem_limit_bytes=52 * 1024 * 1024
        ),
        cost_estimate=pl.CostEstimate(flops=7 * 10**9, bytes_accessed=2 * 10**7, transcendentals=0),
    )(ids, gates, grad_t, acts, weight_t)


def on_device(grad_out, route_ids, route_gates, hidden_acts, down_weight):
    weight_grad, hidden_grad = routed_backward(
        route_ids.T, route_gates.T, grad_out.T, hidden_acts[0, 0], down_weight[0].T
    )
    block = hidden_acts.shape[3] // lax.axis_size("dp")
    shift = weight_grad.shape[1] - block
    odd = lax.rem(lax.axis_index("dp"), 2) == 1
    weight_grad = jnp.where(odd, weight_grad[:, shift:], weight_grad[:, :block])
    return weight_grad.T[None], hidden_grad.T[None, None]


def solution(mesh):
    return jax.shard_map(
        on_device,
        mesh=mesh,
        in_specs=(
            P(("dp", "expert"), "tensor"),
            P(("dp", "expert"), None),
            P(("dp", "expert"), None),
            P("dp", "expert", None, None),
            P("expert", None, "tensor"),
        ),
        out_specs=(P("expert", "dp", "tensor"), P("dp", "expert", None, "tensor")),
        check_vma=False,
    )
```

time: 209 us -> 77.5 us (0.37)
  waiting for transfers between devices: 122 us -> 0 us
  Pallas kernels: 0 us -> 72.3 us
  blocking collectives: 37.2 us -> 0 us
  local copies, waits for them, and re-layouts: 20.2 us -> 2.94 us
  between operations: 14.1 us -> 0.66 us
  matrix products: 13.2 us -> 0 us
    unnamed x4 -> x0, waiting for transfers between devices: 122 us -> none
    pallas_call x0 -> x1, Pallas kernels: none -> 72.3 us  [routed_backward(): pl.pallas_call(kernel, out_shape=(jax.ShapeDtypeStruct((features, 2 * wid...]
    all_to_all x1 -> x0, blocking collectives: 37.2 us -> none  [on_device(): lax.all_to_all(outgoing, 'expert', split_axis=0, concat_axis=0, tiled=True)]
    unnamed x8 -> x7, local copies, waits for them, and re-layouts: 18.6 us -> 2.94 us
    dot_general x3 -> x0, matrix products: 13.2 us -> none  [the longest x1 6.57 us: on_device(): lax.dot_general(activations, arrived, (((0,), (0,)), ((), ())), preferred...]
  transfers between devices with their start and end apart: 2 -> 0, of which waited for: 2 -> 0; matrix products, arithmetic and copies ran while one was open for 8% -> 0% of each run, Pallas kernels for 0% -> 0%
where the time goes in v1:
time: 77.5 us; the launch traced here: 77.3 us
  Pallas kernels  72.3 us (93%)
  local copies, waits for them, and re-layouts  2.94 us (4%)
  other arithmetic  1.4 us (2%)
    pallas_call x1, Pallas kernels, routed_backward(): pl.pallas_call(kernel, out_shape=(jax.ShapeDtypeStruct((features, 2 * wid...  72.3 us
    unnamed x7, local copies, waits for them, and re-layouts  2.94 us

profile of v1, /device:TPU:1, one launch (start us, length us, event | category | flops | bytes accessed | tf_op | source)
XLA Modules:
  0.0 77.3 jit_solution(16578425162484439732)
XLA Ops:
  0.6 0.0 copy-start
  0.6 0.9 %copy-done = bf16[128,448]{0,1:T(8,128)(2,1)S(1)} copy-done((bf16[128,448]{0,1:T(8,128)(2,1)S(1)}, bf16[128,448]{0,1:T(8,128)(2,1)}, u32[]{:S(2)}) %copy-start) | copy-done | bytes 114712
  1.5 0.0 copy-start.1
  1.5 0.7 copy-done.1
  2.2 0.0 copy-start.2
  2.2 0.7 copy-done.2
  2.9 72.3 %shard_map.68 = (bf16[448,1280]{1,0:T(8,128)(2,1)S(1)}, bf16[304,384]{1,0:T(8,128)(2,1)S(1)}) custom-call(s32[2,128]{1,0:T(2,128)S(1)} %bitcast.16, f32[2,128]{1,0:T(2,128)S(1)} %bitcast.17, bf16[448,128]{1,0:T(8,128)(2,1)S(1)} %bitcast.15, bf16[384,4864]{1,0:T(8,128)(2,1)} %bitcast.19, bf16[448,4864]{1,0:T(8,128)(2,1)} %bitcast.18), custom_call_target="tpu_custom_call" | custom-call | flops 7000000000 | bytes 20000000 | tf_op jit(solution)/shard_map/pallas_call | solution.py:374
  75.2 1.4 %select_bitcast_fusion = bf16[1,1216,448]{1,2,0:T(8,128)(2,1)} fusion(bf16[448,1280]{1,0:T(8,128)(2,1)S(1)} %get-tuple-element.4, pred[]{:T(512)S(6)} %eq.3), kind=kLoop, calls=%fused_computation | loop fusion | flops 544768 | bytes 3268609 | tf_op jit(solution)/shard_map/broadcast_in_dim | solution.py:398
  76.6 0.7 copy.8
Async XLA Ops:
  0.6 0.9 %copy-start = (bf16[128,448]{0,1:T(8,128)(2,1)S(1)}, bf16[128,448]{0,1:T(8,128)(2,1)}, u32[]{:S(2)}) copy-start(bf16[128,448]{0,1:T(8,128)(2,1)} %param.5) | copy-start | bytes 344068
  1.5 0.7 copy-start.1
  2.2 0.7 copy-start.2

commit v2 on v1

--- a/solution.py
+++ b/solution.py
@@ -18,12 +18,13 @@
 
 
 def kernel(
-    ids, gates, grad_t, acts, weight_t, gw_out, gh_out,
-    staged, weight, acts_buf, fwd, outgoing, arrived, rows32, named, perm, total,
-    rt0, rt1, peers0, peers1, own0, own1, give0, give1, take0, take1,
-    pa0, pa1, pb0, pb1, ma0, ma1, mb0, mb1,
-    send_sems, recv_sems, local_sems,
+    ids_in, gates_in, grad_in, acts, weight_t, gw, gh,
+    ids, gates, grad_t, staged, weight, acts_buf, fwd, outgoing, arrived, rows32, named, perm, total, done,
+    *rest,
 ):
+    ng = len(GROUPS)
+    rt, peers, own, give, take, pa, pb, ma, mb = (rest[ng * i : ng * i + ng] for i in range(9))
+    send_sems, recv_sems, local_sems = rest[9 * ng :]
     nx, nz, nt = lax.axis_size("dp"), lax.axis_size("expert"), lax.axis_size("tensor")
     ny = nt // 2
     x, z, t = lax.axis_index("dp"), lax.axis_index("expert"), lax.axis_index("tensor")
@@ -35,8 +36,6 @@
     chunk = weight.shape[0] // nt
     part_a = (chunk // 2 + 15) // 16 * 16
     rows_a, rows_b = pl.ds(0, part_a), pl.ds(part_a, chunk - part_a)
-    rt, peers, own, give, take = (rt0, rt1), (peers0, peers1), (own0, own1), (give0, give1), (take0, take1)
-    pa, pb, ma, mb = (pa0, pa1), (pb0, pb1), (ma0, ma1), (mb0, mb1)
     count = [0]
     started = []
 
@@ -52,6 +51,9 @@
         copy.start()
         started.append(copy)
 
+    small = [pltpu.make_async_copy(src, dst, local_sems.at[3 + i]) for i, (src, dst) in enumerate(((ids_in, ids), (gates_in, gates), (grad_in, grad_t)))]
+    for load in small:
+        load.start()
     width = acts_buf.shape[3]
     load_weight = pltpu.make_async_copy(weight_t, staged, local_sems.at[0])
     load_weight.start()
@@ -71,6 +73,8 @@
     for device in greeted:
         pl.semaphore_signal(barrier, inc=1, device_id=device, device_id_type=MESH)
 
+    for load in small:
+        load.wait()
     id0, id1 = ids[0:1, :], ids[1:2, :]
     gate0, gate1 = gates[0:1, :], gates[1:2, :]
     tokens = ids.shape[1]
@@ -134,12 +138,8 @@
 
     load_weight.wait()
 
-    def turn(i, carry):
-        at = pl.multiple_of(i * 128, 128)
-        weight[pl.ds(at, 128), :] = staged[:, pl.ds(at, 128)].astype(F32).T.astype(BF)
-        return carry
-
-    lax.fori_loop(0, weight.shape[0] // 128, turn, 0)
+    for at in range(0, weight.shape[0], 256):
+        weight[at : at + 256, :] = staged[:, at : at + 256].T
 
     slot_count = perm.shape[1]
     stands = lax.broadcasted_iota(jnp.int32, (CAP, slot_count), 1) - lax.broadcasted_iota(jnp.int32, (CAP, slot_count), 0)
@@ -239,32 +239,18 @@
         own[g][i, rows, :] = (own[g][i, rows, :].astype(F32) + buffer[s].astype(F32)).astype(BF)
         start(ring[name, s + 1])
 
-    def stage0(g):
-        prepare(g, 0, 1, 2)
+    def launch(g):
+        ring = rings[g]
         join(g, 0)
-        start(rings[g]["pa", 0])
-        start(rings[g]["mb", 0])
+        start(ring["pa", 0])
+        start(ring["mb", 0])
         join(g, 1, 2)
-        start(rings[g]["pb", 0])
-        start(rings[g]["ma", 0])
-
-    def stage1(g):
-        prepare(g, 3, 4)
-        join(g, 3, 4)
-        for name in ("pa", "mb", "pb", "ma"):
-            step(g, name, 0)
-
-    def stage2(g):
-        prepare(g, 5, 6)
-        join(g, 5, 6)
-        for name in ("pa", "mb", "pb", "ma"):
-            step(g, name, 1)
-
-    def stage3(g):
-        prepare(g, 7)
-        join(g, 7)
-        step(g, "pa", 2)
-        step(g, "mb", 2)
+        start(ring["pb", 0])
+        start(ring["ma", 0])
+
+    def advance(g, s):
+        for name in ("pa", "mb") if s == 2 else ("pa", "mb", "pb", "ma"):
+            step(g, name, s)
 
     def finish(g):
         low, size = GROUPS[g]
@@ -274,11 +260,11 @@
         i = index[0]
         share_a = own[g][i, rows_a, :].astype(F32) + (pa[g][3].astype(F32) + ma[g][2].astype(F32))
         share_b = own[g][i, rows_b, :].astype(F32) + (pb[g][2].astype(F32) + mb[g][3].astype(F32))
-        return jnp.concatenate([share_a, share_b], axis=0).astype(BF)
+        done[:, low : low + size] = jnp.concatenate([share_a, share_b], axis=0).astype(BF)
 
     def weight_grad(q):
         both = [r[...] for r in rt] if q == 0 else [r[q - 1] for r in peers]
-        ordered = sum(dot(b, perm[low : low + size, :]) for b, (low, size) in zip(both, GROUPS)).astype(BF)
+        ordered = dot(jnp.concatenate(both, axis=1), perm[...]).astype(BF)
         for half in range(2):
             columns = pl.ds(half * width, width)
             added = dot(ordered, acts_buf[q, half])
@@ -287,49 +273,53 @@
             elif q < 3:
                 total[:, columns] += added
             else:
-                gw_out[:, columns] = (total[:, columns] + added).astype(BF)
+                gw[:, columns] = (total[:, columns] + added).astype(BF)
 
     near_acts()
+    collect(0)
+    prepare(0, 0, 1, 2, 3, 4)
     half_acts()
-    collect(0)
-    stage0(0)
-    far_acts()
-    stage1(0)
+    launch(0)
+    prepare(0, 5, 6, 7)
+    join(0, 3, 4)
     shared_acts(1)
     shared_acts(2)
-    stage2(0)
+    advance(0, 0)
+    join(0, 5, 6, 7)
     pass_on(0)
+    far_acts()
     collect(1)
     prepare(1, 0, 1, 2)
-    stage3(0)
-    join(1, 0)
-    start(rings[1]["pa", 0])
-    start(rings[1]["mb", 0])
-    join(1, 1, 2)
-    start(rings[1]["pb", 0])
-    start(rings[1]["ma", 0])
-    shared_acts(3)
-    pass_on(1)
-    stage1(1)
-    done0 = finish(0)
-    gh = dot(done0, perm[0 : GROUPS[0][1], :])
-    stage2(1)
+    advance(0, 1)
+    prepare(1, 3, 4)
+    launch(1)
+    prepare(1, 5, 6, 7)
+    advance(0, 2)
+    join(1, 3, 4)
     for load in loads:
         load.wait()
     weight_grad(0)
-    stage3(1)
-    for q in (1, 2):
-        for k in range(3):
-            twin_part[q, k].wait_recv()
-        weight_grad(q)
-    done1 = finish(1)
-    gh_out[...] = (gh + dot(done1, perm[GROUPS[1][0] :, :])).astype(BF)
+    pass_on(1)
+    shared_acts(3)
+    advance(1, 0)
+    join(1, 5, 6, 7)
+    finish(0)
+    for k in range(3):
+        twin_part[1, k].wait_recv()
+    weight_grad(1)
+    advance(1, 1)
+    for k in range(3):
+        twin_part[2, k].wait_recv()
+    weight_grad(2)
+    advance(1, 2)
     for k in range(3):
         twin_part[3, k].wait_recv()
-    for g in range(len(GROUPS)):
+    for g in range(ng):
         for k in range(2):
             to_peers[g][2 + k].wait_recv()
     weight_grad(3)
+    finish(1)
+    gh[...] = dot(done[...], perm[...]).astype(BF)
     for copy in started:
         copy.wait_send()
 
@@ -346,6 +336,9 @@
     sizes = [size for _, size in GROUPS]
     vmem = pltpu.VMEM
     scratch = [
+        vmem(ids.shape, ids.dtype),
+        vmem(gates.shape, gates.dtype),
+        vmem(grad_t.shape, grad_t.dtype),
         vmem((features, hidden), BF),
         vmem((hidden, features), BF),
         vmem((nx, 2, slots, width), BF),
@@ -356,6 +349,7 @@
         vmem((nz, ids.shape[1]), F32),
         vmem((slots, slots), BF),
         vmem((features, 2 * width), F32),
+        vmem((chunk, slots), BF),
     ]
     scratch += [vmem((features, n), BF) for n in sizes]
     scratch += [vmem((3, features, n), BF) for n in sizes]
@@ -363,22 +357,21 @@
         scratch += [vmem((nt // 2, chunk, n), BF) for n in sizes]
     for hops, rows in ((4, part_a), (3, part_b), (3, part_a), (4, part_b)):
         scratch += [vmem((hops, rows, n), BF) for n in sizes]
-    copies = (nz - 1) + 6 + 15 + 8 + 2 * (nt // 2 + 14)
+    copies = (nz - 1) + 6 + 15 + len(GROUPS) * (4 + nt // 2 + 14)
     scratch += [
         pltpu.SemaphoreType.DMA((copies,)),
         pltpu.SemaphoreType.DMA((copies,)),
-        pltpu.SemaphoreType.DMA((3,)),
+        pltpu.SemaphoreType.DMA((6,)),
     ]
-    whole = pl.BlockSpec(memory_space=pltpu.VMEM)
-    away = pl.BlockSpec(memory_space=pl.ANY)
+    away = pl.BlockSpec(memory_space=pltpu.HBM)
     return pl.pallas_call(
         kernel,
         out_shape=(
             jax.ShapeDtypeStruct((features, 2 * width), BF),
             jax.ShapeDtypeStruct((chunk, slots), BF),
         ),
-        in_specs=[whole, whole, whole, away, away],
-        out_specs=(whole, whole),
+        in_specs=[away] * 5,
+        out_specs=(pl.BlockSpec(memory_space=pltpu.VMEM),) * 2,
         scratch_shapes=scratch,
         compiler_params=pltpu.CompilerParams(
             collective_id=0, has_side_effects=True, vmem_limit_bytes=52 * 1024 * 1024

time: 77.5 us -> 73.5 us (0.948)
  the two profiles are of different devices: /device:TPU:1 before, /device:TPU:128 now
where the time goes in v2:
time: 73.5 us; the launch traced here: 73.3 us
  Pallas kernels  68.3 us (93%)
  local copies, waits for them, and re-layouts  2.94 us (4%)
  other arithmetic  1.4 us (2%)
    pallas_call x1, Pallas kernels, routed_backward(): pl.pallas_call(kernel, out_shape=(jax.ShapeDtypeStruct((features, 2 * wid...  68.3 us
    unnamed x7, local copies, waits for them, and re-layouts  2.94 us

profile of v2, /device:TPU:128, one launch (start us, length us, event | category | flops | bytes accessed | tf_op | source)
XLA Modules:
  0.0 73.3 jit_solution(8065514021828495966)
XLA Ops:
  0.6 0.0 copy-start
  0.6 0.9 %copy-done = bf16[128,448]{0,1:T(8,128)(2,1)S(1)} copy-done((bf16[128,448]{0,1:T(8,128)(2,1)S(1)}, bf16[128,448]{0,1:T(8,128)(2,1)}, u32[]{:S(2)}) %copy-start) | copy-done | bytes 114712
  1.5 0.0 copy-start.1
  1.5 0.7 copy-done.1
  2.2 0.0 copy-start.2
  2.2 0.7 copy-done.2
  2.9 68.3 %shard_map.68 = (bf16[448,1280]{1,0:T(8,128)(2,1)S(1)}, bf16[304,384]{1,0:T(8,128)(2,1)S(1)}) custom-call(s32[2,128]{1,0:T(2,128)S(1)} %bitcast.16, f32[2,128]{1,0:T(2,128)S(1)} %bitcast.17, bf16[448,128]{1,0:T(8,128)(2,1)S(1)} %bitcast.15, bf16[384,4864]{1,0:T(8,128)(2,1)} %bitcast.19, bf16[448,4864]{1,0:T(8,128)(2,1)} %bitcast.18), custom_call_target="tpu_custom_call" | custom-call | flops 7000000000 | bytes 20000000 | tf_op jit(solution)/shard_map/pallas_call | solution.py:367
  71.2 1.4 %select_bitcast_fusion = bf16[1,1216,448]{1,2,0:T(8,128)(2,1)} fusion(bf16[448,1280]{1,0:T(8,128)(2,1)S(1)} %get-tuple-element.4, pred[]{:T(512)S(6)} %eq.3), kind=kLoop, calls=%fused_computation | loop fusion | flops 544768 | bytes 3268609 | tf_op jit(solution)/shard_map/broadcast_in_dim | solution.py:391
  72.6 0.7 copy.8
Async XLA Ops:
  0.6 0.9 %copy-start = (bf16[128,448]{0,1:T(8,128)(2,1)S(1)}, bf16[128,448]{0,1:T(8,128)(2,1)}, u32[]{:S(2)}) copy-start(bf16[128,448]{0,1:T(8,128)(2,1)} %param.5) | copy-start | bytes 344068
  1.5 0.7 copy-start.1
  2.2 0.7 copy-start.2
